TPU v7x, 256 devices: a whole 4x4x8 slice. The times are simulated.
256 devices in a mesh: doc: 16 (over z_lo, x), head: 8 (over z_hi, y), cuts: 2 (over core).
Axes of the slice: x: 4, y: 4, z: 8 (z_hi: 2, z_lo: 4; z = z_hi * 4 + z_lo), core: 2. Of those that a mesh axis runs over, the one named last changes fastest.
Arguments:
- inputs: bfloat16 [2, 16, 256, 4096], P('cuts', 'doc'), may hold values from -9 to 9
- weight_query: bfloat16 [4096, 2048], P(None, 'head'), may hold values from -1 to 1
- weight_key: bfloat16 [4096, 2048], P(None, 'head'), may hold values from -2 to 2
- weight_value: bfloat16 [4096, 2048], P(None, 'head'), may hold values from -0.09375 to 0.09375
- grad_output: bfloat16 [2, 16, 256, 2048], P('cuts', 'doc', None, 'head'), may hold values from -24 to 24
- partner_one: int32 [2, 16], P('cuts'), may hold values from 0 to 15, each once within a row
- partner_two: int32 [2, 16], P('cuts'), may hold values from 0 to 15, each once within a row
Outputs:
- grad_key: bfloat16 [2, 16, 256, 2048], P('cuts', 'doc', None, 'head')
- grad_value: bfloat16 [2, 16, 256, 2048], P('cuts', 'doc', None, 'head')
- grad_weight_query: float32 [4096, 2048], P(('doc', 'cuts'), 'head')
- grad_weight_key: float32 [4096, 2048], P(('doc', 'cuts'), 'head')
- grad_weight_value: float32 [4096, 2048], P(('doc', 'cuts'), 'head')
- grad_input: bfloat16 [2, 16, 4096, 256], P('cuts', 'doc', 'head')
Inputs may be any that keep to these rules, and one draw needn't show every extreme that they name: `partner_one`: each row is a permutation of the documents 0 to 15 of the slice. `partner_two`: each row is a permutation of the documents 0 to 15 of the slice.
All inputs are finite; a program needn't handle non-finite values.
Results may differ from a plain program's by a relative error of at most 0.033.
Values may be sent and summed in bfloat16 or wider, within the bound.
No kernel may reach another device: no remote copies, remote signals or barrier semaphores. Data moves between devices by JAX's collectives and lax.ppermute only.
A program may use at most 128 MiB of HBM per device.

v0:
```python
import math
import jax
import jax.numpy as jnp
from jax import lax
from jax.sharding import PartitionSpec as P

HD = 128


def per_device(
    inputs, weight_query, weight_key, weight_value, grad_output, partner_one, partner_two
):
    tokens = inputs[0, 0]
    length = tokens.shape[0]
    columns = weight_query.shape[1]
    head_count = columns // HD
    factor = 1.0 / math.sqrt(HD)
    doc_peers = lax.axis_size("doc")
    block_rows = length // doc_peers
    myself = lax.axis_index("doc")
    first_partner = partner_one[0]
    second_partner = partner_two[0]
    queries = jnp.dot(tokens, weight_query, preferred_element_type=jnp.float32).astype(jnp.bfloat16)
    key_rows = jnp.dot(tokens, weight_key, preferred_element_type=jnp.float32).astype(jnp.bfloat16)
    value_rows = jnp.dot(tokens, weight_value, preferred_element_type=jnp.float32).astype(
        jnp.bfloat16
    )
    key_value = jnp.concatenate([key_rows, value_rows], axis=1)
    chosen = jnp.stack([first_partner[myself], second_partner[myself]])
    offsets = jnp.arange(length, dtype=jnp.int32)
    start_kv = jnp.zeros((2, length, 2 * columns), jnp.bfloat16)
    segment = lax.all_gather(key_value, "doc", axis=0, tiled=True)
    amount = segment.shape[0]
    slot_rows = []
    for which_one in range(2):
        positions = chosen[which_one] * length + offsets
        inside = (positions >= 0) & (positions < amount)
        picked = jnp.take(segment, jnp.clip(positions, 0, amount - 1), axis=0)
        slot_rows.append(jnp.where(inside[:, None], picked, start_kv[which_one]))
    partner_kv = jnp.stack(slot_rows)
    keys_all = jnp.concatenate(
        [key_rows, partner_kv[0, :, :columns], partner_kv[1, :, :columns]], axis=0
    )
    keys_all = keys_all.reshape(3 * length, head_count, HD)
    values_all = jnp.concatenate(
        [value_rows, partner_kv[0, :, columns:], partner_kv[1, :, columns:]], axis=0
    )
    values_all = values_all.reshape(3 * length, head_count, HD)
    query_heads = queries.reshape(length, head_count, HD)
    dout_rows = grad_output[0, 0]
    dout_heads = dout_rows.reshape(length, head_count, HD)
    scores = (
        jnp.einsum("qhe,khe->hqk", query_heads, keys_all, preferred_element_type=jnp.float32)
        * factor
    )
    row_index = lax.broadcasted_iota(jnp.int32, (length, 3 * length), 0)
    col_index = lax.broadcasted_iota(jnp.int32, (length, 3 * length), 1)
    allowed = (col_index >= length) | (col_index <= row_index)
    scores = jnp.where(allowed[None], scores, -jnp.inf)
    maximum = jnp.max(scores, axis=-1, keepdims=True)
    exponent = jnp.exp(scores - maximum)
    totals = jnp.sum(exponent, axis=-1, keepdims=True)
    probability = exponent / totals
    rounded = probability.astype(jnp.bfloat16)
    attended = jnp.einsum("hqk,khe->qhe", rounded, values_all, preferred_element_type=jnp.float32)
    row_delta = jnp.sum(dout_heads.astype(jnp.float32) * attended, axis=-1)
    prob_grad = jnp.einsum(
        "qhe,khe->hqk", dout_heads, values_all, preferred_element_type=jnp.float32
    )
    score_grad = (probability * (prob_grad - row_delta.T[:, :, None])).astype(jnp.bfloat16)
    grad_query = (
        jnp.einsum("hqk,khe->qhe", score_grad, keys_all, preferred_element_type=jnp.float32)
        * factor
    )
    grad_query = grad_query.astype(jnp.bfloat16).reshape(length, columns)
    doc_numbers = jnp.arange(doc_peers, dtype=jnp.int32)
    grad_keys = (
        jnp.einsum("hqk,qhe->khe", score_grad, query_heads, preferred_element_type=jnp.float32)
        * factor
    )
    grad_values = jnp.einsum(
        "hqk,qhe->khe", rounded, dout_heads, preferred_element_type=jnp.float32
    )
    both_grads = jnp.concatenate(
        [grad_keys.reshape(3 * length, columns), grad_values.reshape(3 * length, columns)], axis=1
    )
    own_grad = both_grads[:length]
    outbound = both_grads[length:].reshape(2, doc_peers, block_rows, 2 * columns)
    received = lax.all_to_all(
        outbound.astype(jnp.bfloat16), "doc", split_axis=1, concat_axis=1, tiled=True
    ).astype(outbound.dtype)
    chosen_one = (first_partner[:, None] == doc_numbers[None, :]).astype(jnp.float32)
    chosen_two = (second_partner[:, None] == doc_numbers[None, :]).astype(jnp.float32)
    gathered = jnp.einsum("dt,dbf->tbf", chosen_one, received[0], precision=lax.Precision.HIGHEST)
    gathered = gathered + jnp.einsum(
        "dt,dbf->tbf", chosen_two, received[1], precision=lax.Precision.HIGHEST
    )
    returned = (
        lax.all_to_all(
            gathered.astype(jnp.bfloat16), "doc", split_axis=0, concat_axis=0, tiled=True
        )
        .astype(gathered.dtype)
        .reshape(length, 2 * columns)
    )
    kv_grad = own_grad + returned
    grad_key = kv_grad[:, :columns].astype(jnp.bfloat16)
    grad_value = kv_grad[:, columns:].astype(jnp.bfloat16)
    all_grads = jnp.concatenate([grad_query, grad_key, grad_value], axis=1)
    shared = lax.psum_scatter(
        lax.dot_general(
            tokens, all_grads, (((0,), (0,)), ((), ())), preferred_element_type=jnp.float32
        ).astype(jnp.bfloat16),
        ("doc", "cuts"),
        scatter_dimension=0,
        tiled=True,
    ).astype(jnp.float32)
    numbers = (((1,), (1,)), ((), ()))
    result = lax.dot_general(weight_query, grad_query, numbers, preferred_element_type=jnp.float32)
    result = result + lax.dot_general(
        weight_key, grad_key, numbers, preferred_element_type=jnp.float32
    )
    result = result + lax.dot_general(
        weight_value, grad_value, numbers, preferred_element_type=jnp.float32
    )
    input_rows = lax.psum_scatter(
        result.astype(jnp.bfloat16), "head", scatter_dimension=0, tiled=True
    ).astype(jnp.float32)
    return (
        grad_key.reshape(1, 1, length, columns),
        grad_value.reshape(1, 1, length, columns),
        shared[:, :columns],
        shared[:, columns : 2 * columns],
        shared[:, 2 * columns :],
        input_rows.astype(jnp.bfloat16).reshape(1, 1, input_rows.shape[0], length),
    )


def solution(mesh):
    in_specs = (
        P("cuts", "doc", None, None),
        P(None, "head"),
        P(None, "head"),
        P(None, "head"),
        P("cuts", "doc", None, "head"),
        P("cuts", None),
        P("cuts", None),
    )
    out_specs = (
        P("cuts", "doc", None, "head"),
        P("cuts", "doc", None, "head"),
        P(("doc", "cuts"), "head"),
        P(("doc", "cuts"), "head"),
        P(("doc", "cuts"), "head"),
        P("cuts", "doc", "head", None),
    )
    return jax.shard_map(
        per_device, mesh=mesh, in_specs=in_specs, out_specs=out_specs, check_vma=False
    )
```

profile of v0, /device:TPU:16, one launch (start us, length us, event | category | flops | bytes accessed | tf_op | source)
XLA Modules:
  0.0 437.8 jit_solution(7440671462932104760)
XLA Ops:
  7.2 1.5 copy-done
  8.8 2.7 fusion.20
  11.5 1.0 fusion.23
  18.3 2.5 fusion.17
  20.8 84.0 %all-gather.2.cloned.1.call-done = bf16[4096,512]{0,1:T(8,128)(2,1)} async-done(((bf16[256,512]{0,1:T(8,128)(2,1)}), bf16[4096,512]{0,1:T(8,128)(2,1)}) %all-gather.2.cloned.1.call-update) | async-done | bytes 4194320 | tf_op jit(solution)/shard_map/all_gather | solution.py:32
  104.8 6.5 %copy.57 = bf16[4096,512]{1,0:T(8,128)(2,1)} copy(bf16[4096,512]{0,1:T(8,128)(2,1)} %all-gather.2.cloned.1.call-done) | data formatting | bytes 8388608 | tf_op jit(solution)/shard_map/all_gather | solution.py:32
  111.3 3.9 gather_fusion.1
  115.3 3.9 gather_fusion
  121.8 1.9 fusion.63
  123.7 1.6 fusion.29
  125.3 1.2 fusion.65
  126.5 1.4 copy.75
  127.9 1.6 fusion.26
  129.5 1.9 fusion.12
  131.4 0.9 copy-done.5
  132.3 1.2 convolution_multiply_fusion
  133.5 2.3 copy.74
  135.8 1.1 fusion.27
  137.0 19.8 %all_to_all.10 = bf16[2,16,16,512]{3,2,0,1:T(8,128)(2,1)S(1)} all-to-all(bf16[2,16,16,512]{3,2,0,1:T(8,128)(2,1)S(1)} %copy.76), channel_id=1, replica_groups=mesh['doc'=16,'head'=8,'cuts'=2] {'doc'}, dimensions={1} | all-to-all | bytes 1048576 | tf_op jit(solution)/shard_map/all_to_all | solution.py:89
  158.2 3.5 all-to-all-start.1
  162.0 1.6 fusion.16
  163.6 4.3 fusion.64
  167.9 3.8 all-to-all-done.1
  171.7 1.2 fusion.32
  173.4 3.1 convolution_add_fusion.1
  176.5 2.1 fusion.3
  178.7 4.5 %fusion.1 = bf16[4096,768]{0,1:T(8,128)(2,1)} fusion(bf16[1,1,256,4096]{3,2,1,0:T(8,128)(2,1)S(1)} %copy-done, bf16[256,512]{1,0:T(8,128)(2,1)S(1)} %fusion.32, bf16[256,256]{1,0:T(8,128)(2,1)S(1)} %copy.81), kind=kOutput, calls=%fused_computation.4 | convolution fusion | flops 1614544896 | bytes 8781824 | tf_op jit(solution)/shard_map/dot_general | solution.py:110
  183.2 8.6 %copy.91 = bf16[4096,768]{1,0:T(8,128)(2,1)} copy(bf16[4096,768]{0,1:T(8,128)(2,1)} %fusion.1) | data formatting | bytes 12582912
  192.6 81.1 %reduce-scatter.5.cloned.1.call-done = bf16[512,256]{0,1:T(8,128)(2,1)} async-done(((bf16[4096,256]{0,1:T(8,128)(2,1)}), bf16[512,256]{0,1:T(8,128)(2,1)}) %reduce-scatter.5.cloned.1.call-update) | async-done | bytes 262160 | tf_op jit(solution)/shard_map/reduce_scatter | solution.py:125
  273.7 1.8 copy.85
  275.5 152.4 %reduce-scatter.7.cloned.1.call-done = bf16[128,768]{1,0:T(8,128)(2,1)} async-done(((bf16[4096,768]{1,0:T(8,128)(2,1)}), bf16[128,768]{1,0:T(8,128)(2,1)}) %reduce-scatter.7.cloned.1.call-update) | async-done | bytes 196624
  427.9 1.1 copy.92
  (72 shorter events, 13.6 us)
Async XLA Ops:
  7.2 1.6 copy-start
  7.2 97.6 %all-gather.2.cloned.1.call-start = ((), (), s32[]{:S(2)}) async-start(), calls=%async_computation.4 | async-start | bytes 4456448 | tf_op jit(solution)/shard_map/all_gather | solution.py:32
  8.8 2.7 copy-start.2
  11.4 2.0 copy-start.6
  11.5 2.1 copy-start.13
  11.5 2.1 copy-start.14
  13.3 108.5 %copy-start.7 = (bf16[256,2,128]{2,0,1:T(8,128)(2,1)}, bf16[256,2,128]{2,0,1:T(8,128)(2,1)S(1)}, u32[]{:S(2)}) copy-start(bf16[256,2,128]{2,0,1:T(8,128)(2,1)S(1)} %copy.61) | copy-start | bytes 393220
  121.5 2.2 copy-start.9
  121.8 3.5 copy-start.11
  125.3 1.2 copy-start.4
  125.3 2.6 copy-start.12
  131.4 0.9 copy-start.5
  156.8 5.2 %copy-start.8 = (bf16[256,2,128]{2,0,1:T(8,128)(2,1)S(1)}, bf16[256,2,128]{2,0,1:T(8,128)(2,1)}, u32[]{:S(2)}) copy-start(bf16[256,2,128]{2,0,1:T(8,128)(2,1)} %copy-done.7) | copy-start | bytes 393220
  156.8 5.2 %copy-start.10 = (bf16[256,2,128]{2,0,1:T(8,128)(2,1)S(1)}, bf16[256,2,128]{2,0,1:T(8,128)(2,1)}, u32[]{:S(2)}) copy-start(bf16[256,2,128]{2,0,1:T(8,128)(2,1)} %copy-done.9) | copy-start | bytes 393220
  158.2 13.5 %all-to-all-start.1 = ((bf16[16,16,512]{2,1,0:T(8,128)(2,1)}), bf16[16,16,512]{2,1,0:T(8,128)(2,1)S(1)}, u32[]{:S(2)}, u32[]{:S(2)}) async-start(bf16[16,16,512]{2,1,0:T(8,128)(2,1)} %copy.79), calls=%async_computation.1 | async-start | bytes 524288 | tf_op jit(solution)/shard_map/all_to_all | solution.py:99
  161.8 111.9 %reduce-scatter.5.cloned.1.call-start = ((), (), s32[]{:S(2)}) async-start(), calls=%async_computation.5 | async-start | bytes 2359296 | tf_op jit(solution)/shard_map/reduce_scatter | solution.py:125
  171.7 1.7 copy-start.1
  173.4 3.1 copy-start.3
  178.6 249.3 %reduce-scatter.7.cloned.1.call-start = ((), (), s32[]{:S(2)}) async-start(), calls=%async_computation.6 | async-start | bytes 6488064
Sparse Core Ops, SparseCore 0:
  13.3 91.4 all-gather.1
  178.7 94.9 reduce-scatter.4
  276.4 151.4 reduce-scatter.6
where the time goes:
time: 439 us; the launch traced here: 438 us
  waiting for transfers between devices  321 us (73%)
  local copies, waits for them, and re-layouts  39.2 us (9%)
  matrix products  30 us (7%)
  blocking collectives  19.8 us (5%)
  between operations  14.2 us (3%)
  other arithmetic  9.41 us (2%)
    unnamed x4, waiting for transfers between devices  152 us
    all_gather x1, waiting for transfers between devices, per_device(): segment = lax.all_gather(key_value, 'doc', axis=0, tiled=True)  84 us
    reduce_scatter x1, waiting for transfers between devices, per_device(): lax.psum_scatter(result.astype(jnp.bfloat16), 'head', scatter_dimension=0...  81.1 us
    all_to_all x1, blocking collectives, per_device(): lax.all_to_all(outbound.astype(jnp.bfloat16), 'doc', split_axis=1, concat...  19.8 us
    unnamed x37, local copies, waits for them, and re-layouts  16.9 us
  transfers between devices with their start and end apart: 4, of which 4 were waited for; matrix products, arithmetic and copies ran while one was open for 7% of the time, Pallas kernels for 0%

commit v1 on v0

--- a/solution.py
+++ b/solution.py
@@ -86,8 +86,14 @@
     )
     own_grad = both_grads[:length]
     outbound = both_grads[length:].reshape(2, doc_peers, block_rows, 2 * columns)
-    received = lax.all_to_all(
-        outbound.astype(jnp.bfloat16), "doc", split_axis=1, concat_axis=1, tiled=True
+    received = jnp.concatenate(
+        lax.all_to_all(
+            jnp.stack(jnp.split(outbound.astype(jnp.bfloat16), lax.axis_size("doc"), axis=1)),
+            "doc",
+            0,
+            0,
+        ),
+        axis=1,
     ).astype(outbound.dtype)
     chosen_one = (first_partner[:, None] == doc_numbers[None, :]).astype(jnp.float32)
     chosen_two = (second_partner[:, None] == doc_numbers[None, :]).astype(jnp.float32)

time: 439 us -> 439 us (level)
    unnamed x37 -> x52, local copies, waits for them, and re-layouts: 16.9 us -> 17 us
where the time goes in v1:
time: 439 us; the launch traced here: 438 us
  waiting for transfers between devices  321 us (73%)
  local copies, waits for them, and re-layouts  39.5 us (9%)
  matrix products  29.9 us (7%)
  blocking collectives  19.8 us (5%)
  between operations  14.3 us (3%)
  other arithmetic  9.41 us (2%)
    unnamed x4, waiting for transfers between devices  152 us
    all_gather x1, waiting for transfers between devices, per_device(): segment = lax.all_gather(key_value, 'doc', axis=0, tiled=True)  84 us
    reduce_scatter x1, waiting for transfers between devices, per_device(): lax.psum_scatter(result.astype(jnp.bfloat16), 'head', scatter_dimension=0...  81.1 us
    all_to_all x1, blocking collectives, per_device(): lax.all_to_all(jnp.stack(jnp.split(outbound.astype(jnp.bfloat16), lax.axi...  19.8 us
    unnamed x52, local copies, waits for them, and re-layouts  17 us
  transfers between devices with their start and end apart: 4, of which 4 were waited for; matrix products, arithmetic and copies ran while one was open for 7% of the time, Pallas kernels for 0%

profile of v1, /device:TPU:16, one launch (start us, length us, event | category | flops | bytes accessed | tf_op | source)
XLA Modules:
  0.0 437.7 jit_solution(18151598186662684306)
XLA Ops:
  7.2 1.5 copy-done
  8.8 2.7 fusion.20
  11.5 1.0 fusion.23
  18.3 2.5 fusion.17
  20.8 84.0 %all-gather.2.cloned.1.call-done = bf16[4096,512]{0,1:T(8,128)(2,1)} async-done(((bf16[256,512]{0,1:T(8,128)(2,1)}), bf16[4096,512]{0,1:T(8,128)(2,1)}) %all-gather.2.cloned.1.call-update) | async-done | bytes 4194320 | tf_op jit(solution)/shard_map/all_gather | solution.py:32
  104.8 6.5 %copy.129 = bf16[4096,512]{1,0:T(8,128)(2,1)} copy(bf16[4096,512]{0,1:T(8,128)(2,1)} %all-gather.2.cloned.1.call-done) | data formatting | bytes 8388608 | tf_op jit(solution)/shard_map/all_gather | solution.py:32
  111.3 3.9 gather_fusion.1
  115.3 3.9 gather_fusion
  121.8 1.9 fusion.78
  123.7 1.6 fusion.29
  125.3 1.2 fusion.80
  126.5 1.4 copy.147
  127.9 1.6 fusion.26
  129.5 1.9 fusion.12
  131.4 0.9 copy-done.5
  132.3 1.2 convolution_multiply_fusion
  133.5 2.3 copy.146
  135.8 1.1 fusion.27
  137.1 19.8 %all_to_all.10 = bf16[16,2,1,16,512]{4,3,2,1,0:T(8,128)(2,1)S(1)} all-to-all(bf16[16,2,1,16,512]{4,3,2,1,0:T(8,128)(2,1)S(1)} %bitcast.182), channel_id=1, replica_groups=mesh['doc'=16,'head'=8,'cuts'=2] {'doc'}, dimensions={0} | all-to-all | bytes 1048576 | tf_op jit(solution)/shard_map/all_to_all | solution.py:90
  158.5 3.5 all-to-all-start.1
  162.3 1.6 fusion.16
  163.9 4.3 fusion.79
  168.2 3.8 all-to-all-done.1
  172.0 1.2 fusion.32
  173.7 3.1 convolution_add_fusion.1
  176.7 2.1 fusion.3
  179.0 4.5 %fusion.1 = bf16[4096,768]{0,1:T(8,128)(2,1)} fusion(bf16[1,1,256,4096]{3,2,1,0:T(8,128)(2,1)S(1)} %copy-done, bf16[256,512]{1,0:T(8,128)(2,1)S(1)} %fusion.32, bf16[256,256]{1,0:T(8,128)(2,1)S(1)} %copy.152), kind=kOutput, calls=%fused_computation.4 | convolution fusion | flops 1614544896 | bytes 8781824 | tf_op jit(solution)/shard_map/dot_general | solution.py:116
  183.5 8.6 %copy.162 = bf16[4096,768]{1,0:T(8,128)(2,1)} copy(bf16[4096,768]{0,1:T(8,128)(2,1)} %fusion.1) | data formatting | bytes 12582912
  192.9 81.1 %reduce-scatter.5.cloned.1.call-done = bf16[512,256]{0,1:T(8,128)(2,1)} async-done(((bf16[4096,256]{0,1:T(8,128)(2,1)}), bf16[512,256]{0,1:T(8,128)(2,1)}) %reduce-scatter.5.cloned.1.call-update) | async-done | bytes 262160 | tf_op jit(solution)/shard_map/reduce_scatter | solution.py:131
  274.0 1.8 copy.156
  275.8 152.0 %reduce-scatter.7.cloned.1.call-done = bf16[128,768]{1,0:T(8,128)(2,1)} async-done(((bf16[4096,768]{1,0:T(8,128)(2,1)}), bf16[128,768]{1,0:T(8,128)(2,1)}) %reduce-scatter.7.cloned.1.call-update) | async-done | bytes 196624
  427.8 1.1 copy.163
  (87 shorter events, 13.8 us)
Async XLA Ops:
  7.2 1.6 copy-start
  7.2 97.6 %all-gather.2.cloned.1.call-start = ((), (), s32[]{:S(2)}) async-start(), calls=%async_computation.4 | async-start | bytes 4456448 | tf_op jit(solution)/shard_map/all_gather | solution.py:32
  8.8 2.7 copy-start.2
  11.4 2.0 copy-start.6
  11.5 2.1 copy-start.13
  11.5 2.1 copy-start.14
  13.3 108.4 %copy-start.7 = (bf16[256,2,128]{2,0,1:T(8,128)(2,1)}, bf16[256,2,128]{2,0,1:T(8,128)(2,1)S(1)}, u32[]{:S(2)}) copy-start(bf16[256,2,128]{2,0,1:T(8,128)(2,1)S(1)} %copy.133) | copy-start | bytes 393220
  121.5 2.2 copy-start.9
  121.8 3.5 copy-start.11
  125.3 1.2 copy-start.4
  125.3 2.6 copy-start.12
  131.4 0.9 copy-start.5
  156.9 5.4 %copy-start.8 = (bf16[256,2,128]{2,0,1:T(8,128)(2,1)S(1)}, bf16[256,2,128]{2,0,1:T(8,128)(2,1)}, u32[]{:S(2)}) copy-start(bf16[256,2,128]{2,0,1:T(8,128)(2,1)} %copy-done.7) | copy-start | bytes 393220
  156.9 5.4 %copy-start.10 = (bf16[256,2,128]{2,0,1:T(8,128)(2,1)S(1)}, bf16[256,2,128]{2,0,1:T(8,128)(2,1)}, u32[]{:S(2)}) copy-start(bf16[256,2,128]{2,0,1:T(8,128)(2,1)} %copy-done.9) | copy-start | bytes 393220
  158.5 13.5 %all-to-all-start.1 = ((bf16[16,16,512]{2,1,0:T(8,128)(2,1)}), bf16[16,16,512]{2,1,0:T(8,128)(2,1)S(1)}, u32[]{:S(2)}, u32[]{:S(2)}) async-start(bf16[16,16,512]{2,1,0:T(8,128)(2,1)} %copy.150), calls=%async_computation.1 | async-start | bytes 524288 | tf_op jit(solution)/shard_map/all_to_all | solution.py:105
  162.0 112.0 %reduce-scatter.5.cloned.1.call-start = ((), (), s32[]{:S(2)}) async-start(), calls=%async_computation.5 | async-start | bytes 2359296 | tf_op jit(solution)/shard_map/reduce_scatter | solution.py:131
  172.0 1.7 copy-start.1
  173.6 3.1 copy-start.3
  178.9 249.0 %reduce-scatter.7.cloned.1.call-start = ((), (), s32[]{:S(2)}) async-start(), calls=%async_computation.6 | async-start | bytes 6488064
Sparse Core Ops, SparseCore 0:
  13.3 91.4 all-gather.1
  179.0 94.9 reduce-scatter.4
  276.7 151.0 reduce-scatter.6
